TPU v7x, 32 devices: a whole 2x2x4 slice. The times are simulated.
32 devices in a mesh: dp: 4 (over x, core), centre: 8 (over z, y).
Axes of the slice: x: 2, y: 2, z: 4, core: 2. Of those that a mesh axis runs over, the one named last changes fastest.
Arguments:
- samples: bfloat16 [16384, 128], P('dp'), may hold values from -24 to 24
- centres: bfloat16 [16384, 128], P('centre'), may hold values from -6 to 6
- facility_prior_logprob: float32 [16384], P('centre'), may hold values from -2 to 0
Outputs:
- new_centres: float32 [16384, 128], P('centre')
- new_log_prior: float32 [16384], P('centre')
- log_partition: float32 [16384], P('dp')
All inputs are finite; a program needn't handle non-finite values.
Results may differ from a plain program's by a relative error of at most 0.00075.
Values sent between devices are 32-bit elements; how exact they have to be, the bound alone decides.
A program may use at most 128 MiB of HBM per device.

v0:
```python
import jax
import jax.numpy as jnp
from jax import lax
from jax.sharding import PartitionSpec as P

inverse_coolness_beta = 0.0625


def merged(part, axis, combine):
    gathered = jax.tree.map(lambda a: lax.all_gather(a, axis), part)

    def take(source):
        return jax.tree.map(lambda a: lax.dynamic_index_in_dim(a, source, 0, False), gathered)

    return lax.fori_loop(
        1, lax.axis_size(axis), lambda source, state: combine(state, take(source)), take(0)
    )


def block_scores(rows_block, centres, facility_norm_sq, facility_prior_logprob):
    padded_row_width = rows_block.astype(jnp.float32)
    point_norm_sq = jnp.sum(padded_row_width * padded_row_width, axis=1)
    point_facility_inner = lax.dot_general(
        rows_block, centres, (((1,), (1,)), ((), ())), preferred_element_type=jnp.float32
    )
    return (
        facility_prior_logprob[None, :]
        - (point_norm_sq[:, None] - 2.0 * point_facility_inner + facility_norm_sq[None, :])
        * inverse_coolness_beta
    )


def split_blocks(rows):
    count_rows = rows.shape[0]
    block_rows = min(512, count_rows)
    return rows.reshape(count_rows // block_rows, block_rows, rows.shape[1])


def shard_sufficient_statistics(rows, centres, facility_norm_sq, facility_prior_logprob):

    def block_stats(rows_block):
        unnormalised_membership_energy = block_scores(
            rows_block, centres, facility_norm_sq, facility_prior_logprob
        )
        row_max = jnp.max(unnormalised_membership_energy, axis=1)
        row_total = jnp.sum(jnp.exp(unnormalised_membership_energy - row_max[:, None]), axis=1)
        return (row_max, row_total, unnormalised_membership_energy)

    blocks = split_blocks(rows)
    row_max, row_total, scores = lax.map(block_stats, blocks)
    return (row_max.reshape(rows.shape[0]), row_total.reshape(rows.shape[0]), scores, blocks)


def combine_partial(earlier, later):
    joint_max = jnp.maximum(earlier[0], later[0])
    joint_total = earlier[1] * jnp.exp(earlier[0] - joint_max) + later[1] * jnp.exp(
        later[0] - joint_max
    )
    return (joint_max, joint_total)


def accumulate(blocks, scores, partition, running):
    part_blocks = partition.reshape(blocks.shape[0], blocks.shape[1])

    def block_step(state, pieces):
        mass, weighted = state
        rows_block, unnormalised_membership_energy, part_block = pieces
        resp = jnp.exp(unnormalised_membership_energy - part_block[:, None]).astype(jnp.bfloat16)
        mass = mass + jnp.sum(resp, axis=0, dtype=jnp.float32)
        weighted = weighted + lax.dot_general(
            resp, rows_block, (((0,), (0,)), ((), ())), preferred_element_type=jnp.float32
        )
        return ((mass, weighted), None)

    result, unused = lax.scan(block_step, running, (blocks, scores, part_blocks))
    return result


def finish(weighted, mass, centres_wide, denominator):
    new_centres = (weighted + centres_wide) / (mass + 1.0)[:, None]
    new_log_prior = jnp.log((mass + 1.0) / denominator)
    return (new_centres, new_log_prior)


def shards(samples, centres, facility_prior_logprob):
    centres_wide = centres.astype(jnp.float32)
    facility_norm_sq = jnp.sum(centres_wide * centres_wide, axis=1)
    count_rows = samples.shape[0]
    local_centres = centres.shape[0]
    running = (
        jnp.zeros((local_centres,), jnp.float32),
        jnp.zeros((local_centres, samples.shape[1]), jnp.float32),
    )
    row_max, row_total, scores, blocks = shard_sufficient_statistics(
        samples, centres, facility_norm_sq, facility_prior_logprob
    )
    row_max, row_total = merged((row_max, row_total), "centre", combine_partial)
    log_partition = row_max + jnp.log(row_total)
    running = accumulate(blocks, scores, log_partition, running)
    mass, weighted = running
    denominator = float(count_rows * lax.axis_size("dp") + local_centres * lax.axis_size("centre"))
    weighted, mass = lax.psum((weighted, mass), "dp")
    new_centres, new_log_prior = finish(weighted, mass, centres_wide, denominator)
    return (new_centres, new_log_prior, log_partition)


def solution(mesh):
    placed = (P("dp", None), P("centre", None), P("centre"))
    return jax.shard_map(
        shards,
        mesh=mesh,
        in_specs=placed,
        out_specs=(P("centre", None), P("centre"), P("dp")),
        check_vma=False,
    )
```

profile of v0, /device:TPU:0, one launch (start us, length us, event | category | flops | bytes accessed | tf_op | source)
XLA Modules:
  0.0 256.3 jit_solution(12007676365757333894)
XLA Ops:
  7.2 1.4 fusion.11
  8.6 86.2 %while.44 = (s32[]{:T(128)}, f32[8,512]{1,0:T(8,128)S(1)}, f32[8,512]{1,0:T(8,128)S(1)}, f32[8,512,2048]{2,1,0:T(8,128)}, f32[2048]{0:T(1024)}, /*index=5*/bf16[...) while((s32[]{:T(128)}, f32[8,512]{1,0:T(8,128)S(1)}, ...), condition=%wide.region_5.6_spmd, body=%wide.region_1.5_spmd.sunk | while | flops 277019136 | bytes 34376844 | solution.py:50
  9.7 2.2 fusion.20
  11.9 2.0 copy-done
  14.7 4.6 %bitcast_dynamic-update-slice_fusion.2 = f32[8,512,2048]{2,1,0:T(8,128)} fusion(f32[8,512,2048]{2,1,0:T(8,128)} %get-tuple-element.429, s32[]{:T(128)} %get-tuple-element.426, f32[512,2048]{1,0:T(8,128)} %copy-done), kind=kLoop, calls=%fused_computation.clone.1 | loop fusion | bytes 8389120 | tf_op jit(solution)/shard_map/while/body/jit(dynamic_update_index_in_dim)/dynamic_update_slice | solution.py:50
  20.4 2.2 fusion.20
  22.7 2.0 copy-done
  25.5 4.7 %bitcast_dynamic-update-slice_fusion.2 = f32[8,512,2048]{2,1,0:T(8,128)} fusion(f32[8,512,2048]{2,1,0:T(8,128)} %get-tuple-element.429, s32[]{:T(128)} %get-tuple-element.426, f32[512,2048]{1,0:T(8,128)} %copy-done), kind=kLoop, calls=%fused_computation.clone.1 | loop fusion | bytes 8389120 | tf_op jit(solution)/shard_map/while/body/jit(dynamic_update_index_in_dim)/dynamic_update_slice | solution.py:50
  31.2 2.2 fusion.20
  33.5 2.0 copy-done
  36.3 4.7 %bitcast_dynamic-update-slice_fusion.2 = f32[8,512,2048]{2,1,0:T(8,128)} fusion(f32[8,512,2048]{2,1,0:T(8,128)} %get-tuple-element.429, s32[]{:T(128)} %get-tuple-element.426, f32[512,2048]{1,0:T(8,128)} %copy-done), kind=kLoop, calls=%fused_computation.clone.1 | loop fusion | bytes 8389120 | tf_op jit(solution)/shard_map/while/body/jit(dynamic_update_index_in_dim)/dynamic_update_slice | solution.py:50
  42.0 2.2 fusion.20
  44.2 2.0 copy-done
  47.1 4.6 %bitcast_dynamic-update-slice_fusion.2 = f32[8,512,2048]{2,1,0:T(8,128)} fusion(f32[8,512,2048]{2,1,0:T(8,128)} %get-tuple-element.429, s32[]{:T(128)} %get-tuple-element.426, f32[512,2048]{1,0:T(8,128)} %copy-done), kind=kLoop, calls=%fused_computation.clone.1 | loop fusion | bytes 8389120 | tf_op jit(solution)/shard_map/while/body/jit(dynamic_update_index_in_dim)/dynamic_update_slice | solution.py:50
  52.8 2.2 fusion.20
  55.0 2.0 copy-done
  57.8 4.6 %bitcast_dynamic-update-slice_fusion.2 = f32[8,512,2048]{2,1,0:T(8,128)} fusion(f32[8,512,2048]{2,1,0:T(8,128)} %get-tuple-element.429, s32[]{:T(128)} %get-tuple-element.426, f32[512,2048]{1,0:T(8,128)} %copy-done), kind=kLoop, calls=%fused_computation.clone.1 | loop fusion | bytes 8389120 | tf_op jit(solution)/shard_map/while/body/jit(dynamic_update_index_in_dim)/dynamic_update_slice | solution.py:50
  63.6 2.2 fusion.20
  65.8 2.0 copy-done
  68.6 4.7 %bitcast_dynamic-update-slice_fusion.2 = f32[8,512,2048]{2,1,0:T(8,128)} fusion(f32[8,512,2048]{2,1,0:T(8,128)} %get-tuple-element.429, s32[]{:T(128)} %get-tuple-element.426, f32[512,2048]{1,0:T(8,128)} %copy-done), kind=kLoop, calls=%fused_computation.clone.1 | loop fusion | bytes 8389120 | tf_op jit(solution)/shard_map/while/body/jit(dynamic_update_index_in_dim)/dynamic_update_slice | solution.py:50
  74.3 2.2 fusion.20
  76.6 2.0 copy-done
  79.4 4.7 %bitcast_dynamic-update-slice_fusion.2 = f32[8,512,2048]{2,1,0:T(8,128)} fusion(f32[8,512,2048]{2,1,0:T(8,128)} %get-tuple-element.429, s32[]{:T(128)} %get-tuple-element.426, f32[512,2048]{1,0:T(8,128)} %copy-done), kind=kLoop, calls=%fused_computation.clone.1 | loop fusion | bytes 8389120 | tf_op jit(solution)/shard_map/while/body/jit(dynamic_update_index_in_dim)/dynamic_update_slice | solution.py:50
  85.1 2.2 fusion.20
  87.3 2.0 copy-done
  90.2 4.6 %bitcast_dynamic-update-slice_fusion.2 = f32[8,512,2048]{2,1,0:T(8,128)} fusion(f32[8,512,2048]{2,1,0:T(8,128)} %get-tuple-element.429, s32[]{:T(128)} %get-tuple-element.426, f32[512,2048]{1,0:T(8,128)} %copy-done), kind=kLoop, calls=%fused_computation.clone.1 | loop fusion | bytes 8389120 | tf_op jit(solution)/shard_map/while/body/jit(dynamic_update_index_in_dim)/dynamic_update_slice | solution.py:50
  94.9 32.3 %all-gather = f32[8,1,4096]{2,1,0:T(1,128)S(1)} all-gather(f32[1,1,4096]{2,1,0:T(1,128)S(1)} %reshape.28), channel_id=1, replica_groups=mesh['dp'=4,'centre'=8] {'centre'}, dimensions={0}, use_global_device_ids=true | all-gather | bytes 147456 | tf_op jit(solution)/shard_map/all_gather | solution.py:10
  127.3 30.5 %all-gather.1 = f32[8,1,4096]{2,1,0:T(1,128)S(1)} all-gather(f32[1,1,4096]{2,1,0:T(1,128)S(1)} %reshape.30), channel_id=1, replica_groups=mesh['dp'=4,'centre'=8] {'centre'}, dimensions={0}, use_global_device_ids=true | all-gather | bytes 147456 | tf_op jit(solution)/shard_map/all_gather | solution.py:10
  159.1 49.7 %while.46 = (s32[]{:T(128)}, f32[2048]{0:T(1024)S(1)}, f32[2048,128]{1,0:T(8,128)S(1)}, f32[8,512,2048]{2,1,0:T(8,128)}, f32[8,512]{1,0:T(8,128)S(1)}, /*index=5*/bf16[8,512,128]{2,1,0:T(8,128)(2,1)}, s32[]{:T(128)}, s32[]{:T(128)}) while((s32[]{:T(128)}, f32[2048]{0:T(1024)S(1)}, f32[2048,128]{1,0:T(8,128)S(1)}, ...), condition=%wide.region_10.11_spmd.clone, body=%wide.region_8.10_spmd.clone.sunk | while | flops 275253248 | bytes 10658920 | solution.py:75
  159.1 3.3 %convolution_add_fusion.2 = f32[2048,128]{1,0:T(8,128)S(1)} fusion(f32[8,512,2048]{2,1,0:T(8,128)} %get-tuple-element.489, s32[]{:T(128)} %get-tuple-element.478, f32[512]{0:T(512)S(1)} %bitcast.66, f32[2048,128]{1,0:T(8,128)S(1)} %get-tuple-element.480, pred[]{:T(512)S(6)} %compare.3, bf16[8,512,128]{2,1,0:T(8,128)(2,1)} %get-tuple-element.491), kind=kOutput, calls=%fused_computation.15.clone.1 | convolution fusion | flops 271056896 | bytes 6425601 | tf_op jit(solution)/shard_map/while/body/eval_jaxpr/dot_general | solution.py:70
  162.5 2.8 %convert_reduce_fusion.2 = f32[2048]{0:T(1024)S(1)} fusion(f32[8,512,2048]{2,1,0:T(8,128)} %get-tuple-element.489, s32[]{:T(128)} %get-tuple-element.478, f32[512]{0:T(512)S(1)} %bitcast.67), kind=kLoop, calls=%fused_computation.14.clone.1 | loop fusion | flops 4192256 | bytes 4204548 | tf_op jit(solution)/shard_map/while/body/eval_jaxpr/reduce_sum | solution.py:69
  165.3 3.3 %convolution_add_fusion.2 = f32[2048,128]{1,0:T(8,128)S(1)} fusion(f32[8,512,2048]{2,1,0:T(8,128)} %get-tuple-element.489, s32[]{:T(128)} %get-tuple-element.478, f32[512]{0:T(512)S(1)} %bitcast.66, f32[2048,128]{1,0:T(8,128)S(1)} %get-tuple-element.480, pred[]{:T(512)S(6)} %compare.3, bf16[8,512,128]{2,1,0:T(8,128)(2,1)} %get-tuple-element.491), kind=kOutput, calls=%fused_computation.15.clone.1 | convolution fusion | flops 271056896 | bytes 6425601 | tf_op jit(solution)/shard_map/while/body/eval_jaxpr/dot_general | solution.py:70
  168.7 2.8 %convert_reduce_fusion.2 = f32[2048]{0:T(1024)S(1)} fusion(f32[8,512,2048]{2,1,0:T(8,128)} %get-tuple-element.489, s32[]{:T(128)} %get-tuple-element.478, f32[512]{0:T(512)S(1)} %bitcast.67), kind=kLoop, calls=%fused_computation.14.clone.1 | loop fusion | flops 4192256 | bytes 4204548 | tf_op jit(solution)/shard_map/while/body/eval_jaxpr/reduce_sum | solution.py:69
  171.6 3.3 %convolution_add_fusion.2 = f32[2048,128]{1,0:T(8,128)S(1)} fusion(f32[8,512,2048]{2,1,0:T(8,128)} %get-tuple-element.489, s32[]{:T(128)} %get-tuple-element.478, f32[512]{0:T(512)S(1)} %bitcast.66, f32[2048,128]{1,0:T(8,128)S(1)} %get-tuple-element.480, pred[]{:T(512)S(6)} %compare.3, bf16[8,512,128]{2,1,0:T(8,128)(2,1)} %get-tuple-element.491), kind=kOutput, calls=%fused_computation.15.clone.1 | convolution fusion | flops 271056896 | bytes 6425601 | tf_op jit(solution)/shard_map/while/body/eval_jaxpr/dot_general | solution.py:70
  174.9 2.8 %convert_reduce_fusion.2 = f32[2048]{0:T(1024)S(1)} fusion(f32[8,512,2048]{2,1,0:T(8,128)} %get-tuple-element.489, s32[]{:T(128)} %get-tuple-element.478, f32[512]{0:T(512)S(1)} %bitcast.67), kind=kLoop, calls=%fused_computation.14.clone.1 | loop fusion | flops 4192256 | bytes 4204548 | tf_op jit(solution)/shard_map/while/body/eval_jaxpr/reduce_sum | solution.py:69
  177.8 3.3 %convolution_add_fusion.2 = f32[2048,128]{1,0:T(8,128)S(1)} fusion(f32[8,512,2048]{2,1,0:T(8,128)} %get-tuple-element.489, s32[]{:T(128)} %get-tuple-element.478, f32[512]{0:T(512)S(1)} %bitcast.66, f32[2048,128]{1,0:T(8,128)S(1)} %get-tuple-element.480, pred[]{:T(512)S(6)} %compare.3, bf16[8,512,128]{2,1,0:T(8,128)(2,1)} %get-tuple-element.491), kind=kOutput, calls=%fused_computation.15.clone.1 | convolution fusion | flops 271056896 | bytes 6425601 | tf_op jit(solution)/shard_map/while/body/eval_jaxpr/dot_general | solution.py:70
  181.1 2.8 %convert_reduce_fusion.2 = f32[2048]{0:T(1024)S(1)} fusion(f32[8,512,2048]{2,1,0:T(8,128)} %get-tuple-element.489, s32[]{:T(128)} %get-tuple-element.478, f32[512]{0:T(512)S(1)} %bitcast.67), kind=kLoop, calls=%fused_computation.14.clone.1 | loop fusion | flops 4192256 | bytes 4204548 | tf_op jit(solution)/shard_map/while/body/eval_jaxpr/reduce_sum | solution.py:69
  184.0 3.3 %convolution_add_fusion.2 = f32[2048,128]{1,0:T(8,128)S(1)} fusion(f32[8,512,2048]{2,1,0:T(8,128)} %get-tuple-element.489, s32[]{:T(128)} %get-tuple-element.478, f32[512]{0:T(512)S(1)} %bitcast.66, f32[2048,128]{1,0:T(8,128)S(1)} %get-tuple-element.480, pred[]{:T(512)S(6)} %compare.3, bf16[8,512,128]{2,1,0:T(8,128)(2,1)} %get-tuple-element.491), kind=kOutput, calls=%fused_computation.15.clone.1 | convolution fusion | flops 271056896 | bytes 6425601 | tf_op jit(solution)/shard_map/while/body/eval_jaxpr/dot_general | solution.py:70
  187.3 2.8 %convert_reduce_fusion.2 = f32[2048]{0:T(1024)S(1)} fusion(f32[8,512,2048]{2,1,0:T(8,128)} %get-tuple-element.489, s32[]{:T(128)} %get-tuple-element.478, f32[512]{0:T(512)S(1)} %bitcast.67), kind=kLoop, calls=%fused_computation.14.clone.1 | loop fusion | flops 4192256 | bytes 4204548 | tf_op jit(solution)/shard_map/while/body/eval_jaxpr/reduce_sum | solution.py:69
  190.2 3.3 %convolution_add_fusion.2 = f32[2048,128]{1,0:T(8,128)S(1)} fusion(f32[8,512,2048]{2,1,0:T(8,128)} %get-tuple-element.489, s32[]{:T(128)} %get-tuple-element.478, f32[512]{0:T(512)S(1)} %bitcast.66, f32[2048,128]{1,0:T(8,128)S(1)} %get-tuple-element.480, pred[]{:T(512)S(6)} %compare.3, bf16[8,512,128]{2,1,0:T(8,128)(2,1)} %get-tuple-element.491), kind=kOutput, calls=%fused_computation.15.clone.1 | convolution fusion | flops 271056896 | bytes 6425601 | tf_op jit(solution)/shard_map/while/body/eval_jaxpr/dot_general | solution.py:70
  193.5 2.8 %convert_reduce_fusion.2 = f32[2048]{0:T(1024)S(1)} fusion(f32[8,512,2048]{2,1,0:T(8,128)} %get-tuple-element.489, s32[]{:T(128)} %get-tuple-element.478, f32[512]{0:T(512)S(1)} %bitcast.67), kind=kLoop, calls=%fused_computation.14.clone.1 | loop fusion | flops 4192256 | bytes 4204548 | tf_op jit(solution)/shard_map/while/body/eval_jaxpr/reduce_sum | solution.py:69
  196.4 3.3 %convolution_add_fusion.2 = f32[2048,128]{1,0:T(8,128)S(1)} fusion(f32[8,512,2048]{2,1,0:T(8,128)} %get-tuple-element.489, s32[]{:T(128)} %get-tuple-element.478, f32[512]{0:T(512)S(1)} %bitcast.66, f32[2048,128]{1,0:T(8,128)S(1)} %get-tuple-element.480, pred[]{:T(512)S(6)} %compare.3, bf16[8,512,128]{2,1,0:T(8,128)(2,1)} %get-tuple-element.491), kind=kOutput, calls=%fused_computation.15.clone.1 | convolution fusion | flops 271056896 | bytes 6425601 | tf_op jit(solution)/shard_map/while/body/eval_jaxpr/dot_general | solution.py:70
  199.8 2.8 %convert_reduce_fusion.2 = f32[2048]{0:T(1024)S(1)} fusion(f32[8,512,2048]{2,1,0:T(8,128)} %get-tuple-element.489, s32[]{:T(128)} %get-tuple-element.478, f32[512]{0:T(512)S(1)} %bitcast.67), kind=kLoop, calls=%fused_computation.14.clone.1 | loop fusion | flops 4192256 | bytes 4204548 | tf_op jit(solution)/shard_map/while/body/eval_jaxpr/reduce_sum | solution.py:69
  202.6 3.3 %convolution_add_fusion.2 = f32[2048,128]{1,0:T(8,128)S(1)} fusion(f32[8,512,2048]{2,1,0:T(8,128)} %get-tuple-element.489, s32[]{:T(128)} %get-tuple-element.478, f32[512]{0:T(512)S(1)} %bitcast.66, f32[2048,128]{1,0:T(8,128)S(1)} %get-tuple-element.480, pred[]{:T(512)S(6)} %compare.3, bf16[8,512,128]{2,1,0:T(8,128)(2,1)} %get-tuple-element.491), kind=kOutput, calls=%fused_computation.15.clone.1 | convolution fusion | flops 271056896 | bytes 6425601 | tf_op jit(solution)/shard_map/while/body/eval_jaxpr/dot_general | solution.py:70
  206.0 2.8 %convert_reduce_fusion.2 = f32[2048]{0:T(1024)S(1)} fusion(f32[8,512,2048]{2,1,0:T(8,128)} %get-tuple-element.489, s32[]{:T(128)} %get-tuple-element.478, f32[512]{0:T(512)S(1)} %bitcast.67), kind=kLoop, calls=%fused_computation.14.clone.1 | loop fusion | flops 4192256 | bytes 4204548 | tf_op jit(solution)/shard_map/while/body/eval_jaxpr/reduce_sum | solution.py:69
  209.8 5.8 %psum.15 = f32[2048]{0:T(1024)S(1)} all-reduce(f32[2048]{0:T(1024)S(1)} %get-tuple-element.219), channel_id=1, replica_groups=mesh['dp'=4,'centre'=8] {'dp'}, use_global_device_ids=true, to_apply=%region_12.13 | all-reduce | flops 2048 | bytes 16384 | tf_op jit(solution)/shard_map/psum | solution.py:102
  216.2 30.7 %all-reduce.2.cloned.1.call-done = f32[2048,128]{1,0:T(8,128)} async-done(((f32[2048,128]{1,0:T(8,128)}), f32[2048,128]{1,0:T(8,128)}) %all-reduce.2.cloned.1.call-update) | async-done | bytes 1048592 | tf_op jit(solution)/shard_map/psum | solution.py:102
  246.9 2.5 fusion.12
  (93 shorter events, 18.2 us)
Async XLA Ops:
  7.2 239.7 %all-reduce.2.cloned.1.call-start = ((), (), s32[]{:S(2)}) async-start(), calls=%async_computation | async-start | bytes 2097152 | tf_op jit(solution)/shard_map/psum | solution.py:102
  11.9 2.1 copy-start
  22.6 2.1 copy-start
  33.4 2.1 copy-start
  44.2 2.1 copy-start
  55.0 2.1 copy-start
  65.8 2.1 copy-start
  76.5 2.1 copy-start
  87.3 2.1 copy-start
  158.5 0.6 copy-start.3
  158.5 88.4 %copy-start.2 = (bf16[2048,128]{1,0:T(8,128)(2,1)S(1)}, bf16[2048,128]{1,0:T(8,128)(2,1)}, u32[]{:S(2)}) copy-start(bf16[2048,128]{1,0:T(8,128)(2,1)} %get-tuple-element.497) | copy-start | bytes 1572868
  208.8 1.0 copy-start.1
Sparse Core Ops, SparseCore 0:
  209.9 36.9 all-reduce.1
where the time goes:
time: 257 us; the launch traced here: 256 us
  blocking collectives  68.6 us (27%)
  local copies, waits for them, and re-layouts  56.3 us (22%)
  matrix products  44.3 us (17%)
  other arithmetic  41.4 us (16%)
  waiting for transfers between devices  30.7 us (12%)
  between operations  14.2 us (6%)
    all_gather x2, blocking collectives, merged(): gathered = jax.tree.map(lambda a: lax.all_gather(a, axis), part)  62.8 us
    dynamic_update_slice x24, local copies, waits for them, and re-layouts, shard_sufficient_statistics(): row_max, row_total, scores = lax.map(block_stats, blocks)  37.9 us
    psum x1, waiting for transfers between devices, shards(): weighted, mass = lax.psum((weighted, mass), 'dp')  30.7 us
    dot_general x8, matrix products, block_step(): lax.dot_general(resp, rows_block, (((0,), (0,)), ((), ())), preferred_ele...  26.7 us
    reduce_sum x8, other arithmetic, block_step(): mass = mass + jnp.sum(resp, axis=0, dtype=jnp.float32)  22.6 us
    dot_general x8, matrix products, block_scores(): lax.dot_general(rows_block, centres, (((1,), (1,)), ((), ())), preferred_...  17.6 us
    while x16, local copies, waits for them, and re-layouts  16.3 us
    reduce_sum x8, other arithmetic, block_scores(): point_norm_sq = jnp.sum(padded_row_width * padded_row_width, axis=1)  8.42 us
  transfers between devices with their start and end apart: 1, of which 1 were waited for; matrix products, arithmetic and copies ran while one was open for 0% of the time, Pallas kernels for 0%

commit v1 on v0

v1 whole, which is shorter than its diff:
```python
import functools

import jax
import jax.numpy as jnp
from jax import lax
from jax.experimental import pallas as pl
from jax.experimental.pallas import tpu as pltpu
from jax.sharding import PartitionSpec as P

MESH = pl.DeviceIdType.MESH
BETA = 0.0625
LANES = 128
COLS = 256
MOST = 256
GROUPS = 2


def pieces(value):
    first = value.astype(jnp.bfloat16)
    rest = value - first.astype(jnp.float32)
    second = rest.astype(jnp.bfloat16)
    third = (rest - second.astype(jnp.float32)).astype(jnp.bfloat16)
    return first, second, third


def side_columns(value):
    lane = lax.broadcasted_iota(jnp.int32, value.shape, 1)
    first, second, third = (p.astype(jnp.float32) for p in pieces(value))
    zero = jnp.zeros_like(value)
    picked = jnp.where(lane == 0, first, jnp.where(lane == 1, second, jnp.where(lane == 2, third, zero)))
    return picked.astype(jnp.bfloat16)


def column(row):
    return jnp.broadcast_to(row, (LANES, LANES)).T


def kernel(
    C, D, x_ref, c_ref, p_ref, out_ref, lp_ref,
    caug, e_ref, xw, score_a, score_b, m_ref, sn_ref, stats, own, send_a, recv_a, recv_b,
    stat_send, stat_recv, a_send, a_recv, b_send, b_recv, c_send, c_recv,
):
    n, k = x_ref.shape[0], c_ref.shape[0]
    X = D // 2
    CHUNK = min(MOST, k // 2)
    H = k // CHUNK // 2
    me_c, me_d = lax.axis_index("centre"), lax.axis_index("dp")
    core, mine_x = lax.rem(me_d, 2), lax.div(me_d, 2)
    sibling = mine_x * 2 + (1 - core)

    def far(q):
        return lax.rem(mine_x + q, X) * 2 + core

    barrier = pltpu.get_barrier_semaphore()

    def greet(q, unused):
        pl.semaphore_signal(
            barrier, inc=1, device_id={"centre": lax.rem(me_c + q, C)}, device_id_type=MESH
        )
        return unused

    lax.fori_loop(1, C, greet, 0)
    pl.semaphore_signal(barrier, inc=1, device_id={"dp": sibling}, device_id_type=MESH)
    for q in range(1, X):
        pl.semaphore_signal(barrier, inc=1, device_id={"dp": far(q)}, device_id_type=MESH)

    def widen(b, unused):
        rows = pl.ds(pl.multiple_of(b * LANES, LANES), LANES)
        c = c_ref[rows, :].astype(jnp.float32)
        norm = jnp.sum(c * c, axis=1, keepdims=True)
        bias = column(p_ref[pl.ds(b, 1), :]) - norm * BETA
        caug[rows, :LANES] = (c * (2.0 * BETA)).astype(jnp.bfloat16)
        caug[rows, LANES:] = side_columns(bias)
        return unused

    lax.fori_loop(0, k // LANES, widen, 0)

    KB = min(512, k)
    steps = n // COLS
    ones = jnp.ones((COLS, LANES), jnp.bfloat16)

    def fold(s, op):
        return op(s.reshape(s.shape[0] // 8, 8, COLS), axis=0)

    def score_block(x_rows, kb):
        return lax.dot_general(
            caug[kb * KB:(kb + 1) * KB, :], x_rows, (((1,), (1,)), ((), ())),
            preferred_element_type=jnp.float32,
        )

    def x_of(j):
        rows = pl.ds(pl.multiple_of(j * COLS, COLS), COLS)
        return jnp.concatenate([x_ref[rows, :], ones], axis=1)

    def first_scores(ref, j):
        xr = x_of(j)
        top = None
        for kb in range(k // KB):
            s = score_block(xr, kb)
            ref[kb * KB:(kb + 1) * KB, :] = s
            part = fold(s, jnp.max)
            top = part if top is None else jnp.maximum(top, part)
        return jnp.max(top, axis=0, keepdims=True)

    def step(now, later, j, m):
        following = jnp.minimum(j + 1, steps - 1)
        xr = x_of(following)
        cols = pl.ds(pl.multiple_of(j * COLS, COLS), COLS)
        top = total = None
        for kb in range(k // KB):
            rows = slice(kb * KB, (kb + 1) * KB)
            s = score_block(xr, kb)
            later[rows, :] = s
            part = fold(s, jnp.max)
            top = part if top is None else jnp.maximum(top, part)
            e = jnp.exp(now[rows, :] - m)
            part = fold(e, jnp.sum)
            total = part if total is None else total + part
            e_ref[rows, cols] = e.astype(jnp.bfloat16)
        lse = m + jnp.log(jnp.sum(total, axis=0, keepdims=True))
        xf = x_ref[cols, :].astype(jnp.float32)
        norm = jnp.sum((xf * xf).T, axis=0, keepdims=True)
        for b in range(COLS // LANES):
            row = pl.ds(j * (COLS // LANES) + b, 1)
            part = slice(b * LANES, (b + 1) * LANES)
            m_ref[row, :] = m[:, part]
            sn_ref[row, :] = norm[:, part]
            stats[0, row, :] = lse[:, part]
        return jnp.max(top, axis=0, keepdims=True)

    def pair(i, m):
        m = step(score_a, score_b, 2 * i, m)
        return step(score_b, score_a, 2 * i + 1, m)

    R = n // LANES
    GR = R // GROUPS

    def stat_copy(g, q):
        rows = slice(g * GR, (g + 1) * GR)
        return pltpu.make_async_remote_copy(
            src_ref=stats.at[0, rows], dst_ref=stats.at[q, rows],
            send_sem=stat_send.at[g, q], recv_sem=stat_recv.at[g, q],
            device_id={"centre": lax.rem(me_c + q, C)}, device_id_type=MESH,
        )

    m = first_scores(score_a, 0)
    per_group = steps // 2 // GROUPS
    for g in range(GROUPS):
        m = lax.fori_loop(g * per_group, (g + 1) * per_group, pair, m)
        if g == 0:
            pl.semaphore_wait(barrier, C - 1 + 1 + X - 1)

        def send(q, unused, g=g):
            stat_copy(g, q).start()
            return unused

        lax.fori_loop(1, C, send, 0)

    for g in range(GROUPS):
        def arrive(q, unused, g=g):
            stat_copy(g, q).wait()
            return unused

        lax.fori_loop(1, C, arrive, 0)
        rows = slice(g * GR, (g + 1) * GR)
        top = lax.fori_loop(
            1, C, lambda q, t, rows=rows: jnp.maximum(t, stats[q, rows, :]), stats[0, rows, :]
        )
        total = lax.fori_loop(
            0, C, lambda q, t, rows=rows, top=top: t + jnp.exp(stats[q, rows, :] - top),
            jnp.zeros_like(top),
        )
        lse = top + jnp.log(total)
        lp_ref[rows, :] = lse - sn_ref[rows, :] * BETA
        m_ref[rows, :] = jnp.exp(m_ref[rows, :] - lse)

        def scale(r, unused):
            at = pl.ds(pl.multiple_of(r * LANES, LANES), LANES)
            w = column(m_ref[pl.ds(r, 1), :])
            xw[at, :LANES] = (x_ref[at, :].astype(jnp.float32) * w).astype(jnp.bfloat16)
            xw[at, LANES:] = side_columns(w)
            return unused

        lax.fori_loop(g * GR, (g + 1) * GR, scale, 0)

    def partial(chunk, ref, i):
        rows = pl.ds(pl.multiple_of(chunk * CHUNK, CHUNK), CHUNK)
        s = jnp.dot(e_ref[rows, :], xw[...], preferred_element_type=jnp.float32)
        ref[i, :CHUNK, :] = s[:, :LANES]
        masses = jnp.zeros((8, LANES), jnp.float32)
        line = lax.broadcasted_iota(jnp.int32, (8, LANES), 0)
        for b in range(CHUNK // LANES):
            t = s[b * LANES:(b + 1) * LANES, LANES:].T
            row = jnp.sum(t[0:8, :], axis=0, keepdims=True)
            masses = jnp.where(line == b, jnp.broadcast_to(row, (8, LANES)), masses)
        ref[i, CHUNK:, :] = masses

    def a_copy(i):
        return pltpu.make_async_remote_copy(
            src_ref=send_a.at[i], dst_ref=recv_a.at[i], send_sem=a_send.at[i], recv_sem=a_recv.at[i],
            device_id={"dp": sibling}, device_id_type=MESH,
        )

    def b_copy(q, i):
        return pltpu.make_async_remote_copy(
            src_ref=own.at[i], dst_ref=recv_b.at[q - 1, i],
            send_sem=b_send.at[q - 1, i], recv_sem=b_recv.at[q - 1, i],
            device_id={"dp": far(q)}, device_id_type=MESH,
        )

    def c_copy(half, i):
        return pltpu.make_async_remote_copy(
            src_ref=out_ref.at[half * H + i], dst_ref=out_ref.at[half * H + i],
            send_sem=c_send.at[i], recv_sem=c_recv.at[i],
            device_id={"dp": sibling}, device_id_type=MESH,
        )

    def chip_sum(i):
        a_copy(i).wait()
        own[i] = own[i] + recv_a[i]
        for q in range(1, X):
            b_copy(q, i).start()

    def produce(i, unused):
        partial((1 - core) * H + i, send_a, i)
        a_copy(i).start()
        partial(core * H + i, own, i)
        chip_sum(i)
        return unused

    lax.fori_loop(0, H, produce, 0)

    denominator = float(n * D + k * C)

    def final(i, unused):
        chunk = core * H + i
        for q in range(1, X):
            b_copy(q, i).wait()
        parts = [own[i]] + [recv_b[q - 1, i] for q in range(1, X)]
        total = functools.reduce(lambda a, b: a + b, parts)
        for b in range(CHUNK // LANES):
            rows = pl.ds(pl.multiple_of(chunk * CHUNK, CHUNK) + b * LANES, LANES)
            mass = column(total[CHUNK + b:CHUNK + b + 1, :])
            c = c_ref[rows, :].astype(jnp.float32)
            out_ref[chunk, b * LANES:(b + 1) * LANES, :] = (
                total[b * LANES:(b + 1) * LANES, :] + c
            ) / (mass + 1.0)
        out_ref[chunk, CHUNK:, :] = jnp.log((total[CHUNK:, :] + 1.0) / denominator)
        c_copy(core, i).start()
        return unused

    lax.fori_loop(0, H, final, 0)

    def finish(i, unused):
        c_copy(core, i).wait()
        return unused

    lax.fori_loop(0, H, finish, 0)


def solution(mesh):
    C, D = mesh.shape["centre"], mesh.shape["dp"]

    def shards(samples, centres, prior):
        n, k = samples.shape[0], centres.shape[0]
        CHUNK = min(MOST, k // 2)
        X, H, R = D // 2, k // CHUNK // 2, n // LANES
        vmem = pl.BlockSpec(memory_space=pltpu.VMEM)
        f32, bf16 = jnp.float32, jnp.bfloat16
        dma = pltpu.SemaphoreType.DMA
        chunk = (CHUNK + 8, LANES)
        out, lp = pl.pallas_call(
            functools.partial(kernel, C, D),
            out_shape=(
                jax.ShapeDtypeStruct((2 * H,) + chunk, f32),
                jax.ShapeDtypeStruct((R, LANES), f32),
            ),
            in_specs=[vmem] * 3,
            out_specs=(vmem, vmem),
            scratch_shapes=[
                pltpu.VMEM((k, 2 * LANES), bf16),
                pltpu.VMEM((k, n), bf16),
                pltpu.VMEM((n, 2 * LANES), bf16),
                pltpu.VMEM((k, COLS), f32),
                pltpu.VMEM((k, COLS), f32),
                pltpu.VMEM((R, LANES), f32),
                pltpu.VMEM((R, LANES), f32),
                pltpu.VMEM((C, R, LANES), f32),
                pltpu.VMEM((H,) + chunk, f32),
                pltpu.VMEM((H,) + chunk, f32),
                pltpu.VMEM((H,) + chunk, f32),
                pltpu.VMEM((max(X - 1, 1), H) + chunk, f32),
                dma((GROUPS, C)), dma((GROUPS, C)),
                dma((H,)), dma((H,)),
                dma((max(X - 1, 1), H)), dma((max(X - 1, 1), H)),
                dma((H,)), dma((H,)),
            ],
            compiler_params=pltpu.CompilerParams(
                collective_id=0, has_side_effects=True, vmem_limit_bytes=50 * 2**20
            ),
            cost_estimate=pl.CostEstimate(
                flops=8 * n * k * LANES, bytes_accessed=4 * n * LANES, transcendentals=n * k
            ),
        )(samples, centres, prior.reshape(k // LANES, LANES))
        new_centres = out[:, :CHUNK, :].reshape(k, LANES)
        new_log_prior = out[:, CHUNK:CHUNK + CHUNK // LANES, :].reshape(k)
        return new_centres, new_log_prior, lp.reshape(n)

    return jax.shard_map(
        shards,
        mesh=mesh,
        in_specs=(P("dp", None), P("centre", None), P("centre")),
        out_specs=(P("centre", None), P("centre"), P("dp")),
        check_vma=False,
    )
```

time: 257 us -> 48.2 us (0.19)
  blocking collectives: 68.6 us -> 0 us
  local copies, waits for them, and re-layouts: 56.3 us -> 5.2 us
  matrix products: 44.3 us -> 0 us
  Pallas kernels: 0 us -> 42.1 us
  other arithmetic: 41.4 us -> 0 us
  waiting for transfers between devices: 30.7 us -> 0 us
  between operations: 14.2 us -> 0.65 us
    all_gather x2 -> x0, blocking collectives: 62.8 us -> none  [merged(): gathered = jax.tree.map(lambda a: lax.all_gather(a, axis), part)]
    dot_general x16 -> x0, matrix products: 44.3 us -> none  [the longest x8 26.7 us: block_step(): lax.dot_general(resp, rows_block, (((0,), (0,)), ((), ())), preferred_ele...]
    pallas_call x0 -> x1, Pallas kernels: none -> 42.1 us  [shards(): pl.pallas_call(functools.partial(kernel, C, D), out_shape=(jax.ShapeDtype...]
    reduce_sum x25 -> x0, other arithmetic: 38 us -> none  [the longest x8 22.6 us: block_step(): mass = mass + jnp.sum(resp, axis=0, dtype=jnp.float32)]
    dynamic_update_slice x24 -> x0, local copies, waits for them, and re-layouts: 37.9 us -> none  [shard_sufficient_statistics(): row_max, row_total, scores = lax.map(block_stats, blocks)]
    psum x1 -> x0, waiting for transfers between devices: 30.7 us -> none  [shards(): weighted, mass = lax.psum((weighted, mass), 'dp')]
    while x16 -> x0, local copies, waits for them, and re-layouts: 16.3 us -> none
    psum x1 -> x0, blocking collectives: 5.77 us -> none  [shards(): weighted, mass = lax.psum((weighted, mass), 'dp')]
  transfers between devices with their start and end apart: 1 -> 0, of which waited for: 1 -> 0; matrix products, arithmetic and copies ran while one was open for 0% -> 0% of each run, Pallas kernels for 0% -> 0%
where the time goes in v1:
time: 48.2 us; the launch traced here: 47.9 us
  Pallas kernels  42.1 us (87%)
  local copies, waits for them, and re-layouts  5.2 us (11%)
  between operations  0.65 us (1%)
    pallas_call x1, Pallas kernels, shards(): pl.pallas_call(functools.partial(kernel, C, D), out_shape=(jax.ShapeDtype...  42.1 us
    unnamed x7, local copies, waits for them, and re-layouts  3.56 us
    slice x1, local copies, waits for them, and re-layouts, shards(): new_centres = out[:, :CHUNK, :].reshape(k, LANES)  1.04 us

profile of v1, /device:TPU:0, one launch (start us, length us, event | category | flops | bytes accessed | tf_op | source)
XLA Modules:
  0.0 47.9 jit_solution(11821506672887350769)
XLA Ops:
  0.6 0.0 copy-start
  0.6 1.2 %copy-done = bf16[4096,128]{1,0:T(8,128)(2,1)S(1)} copy-done((bf16[4096,128]{1,0:T(8,128)(2,1)S(1)}, bf16[4096,128]{1,0:T(8,128)(2,1)}, u32[]{:S(2)}) %copy-start) | copy-done | bytes 1048600
  1.9 0.0 copy-start.1
  1.9 1.0 %copy-done.1 = bf16[2048,128]{1,0:T(8,128)(2,1)S(1)} copy-done((bf16[2048,128]{1,0:T(8,128)(2,1)S(1)}, bf16[2048,128]{1,0:T(8,128)(2,1)}, u32[]{:S(2)}) %copy-start.1) | copy-done | bytes 524312
  2.9 0.0 copy-start.2
  2.9 0.7 %copy-done.2 = f32[2048]{0:T(1024)S(1)} copy-done((f32[2048]{0:T(1024)S(1)}, f32[2048]{0:T(1024)}, u32[]{:S(2)}) %copy-start.2) | copy-done | bytes 8216
  3.6 42.1 %shard_map.58 = (f32[8,264,128]{2,1,0:T(8,128)S(1)}, f32[32,128]{1,0:T(8,128)S(1)}) custom-call(bf16[4096,128]{1,0:T(8,128)(2,1)S(1)} %copy-done, bf16[2048,128]{1,0:T(8,128)(2,1)S(1)} %copy-done.1, f32[16,128]{1,0:T(8,128)S(1)} %bitcast.5), custom_call_target="tpu_custom_call" | custom-call | flops 8589934592 | bytes 2097152 | tf_op jit(solution)/shard_map/pallas_call | solution.py:272
  45.7 0.6 %slice.7 = f32[8,2,128]{2,1,0:T(2,128)} slice(f32[8,264,128]{2,1,0:T(8,128)S(1)} %get-tuple-element.5), slice={[0:8], [256:258], [0:128]} | slice | bytes 16384 | tf_op jit(solution)/shard_map/slice | solution.py:306
  46.3 1.0 %slice.6 = f32[8,256,128]{2,1,0:T(8,128)} slice(f32[8,264,128]{2,1,0:T(8,128)S(1)} %get-tuple-element.5), slice={[0:8], [0:256], [0:128]} | slice | bytes 2097152 | tf_op jit(solution)/shard_map/slice | solution.py:305
  47.3 0.6 %copy.7 = f32[4096]{0:T(1024)} copy(f32[4096]{0:T(1024)S(1)} %bitcast.4) | data formatting | bytes 32768
Async XLA Ops:
  0.6 1.2 %copy-start = (bf16[4096,128]{1,0:T(8,128)(2,1)S(1)}, bf16[4096,128]{1,0:T(8,128)(2,1)}, u32[]{:S(2)}) copy-start(bf16[4096,128]{1,0:T(8,128)(2,1)} %x_ref.1) | copy-start | bytes 3145732
  1.9 1.0 %copy-start.1 = (bf16[2048,128]{1,0:T(8,128)(2,1)S(1)}, bf16[2048,128]{1,0:T(8,128)(2,1)}, u32[]{:S(2)}) copy-start(bf16[2048,128]{1,0:T(8,128)(2,1)} %c_ref.1) | copy-start | bytes 1572868
  2.9 0.7 %copy-start.2 = (f32[2048]{0:T(1024)S(1)}, f32[2048]{0:T(1024)}, u32[]{:S(2)}) copy-start(f32[2048]{0:T(1024)} %param.5) | copy-start | bytes 24580

commit v2 on v1

--- a/solution.py
+++ b/solution.py
@@ -1,4 +1,5 @@
 import functools
+import math
 
 import jax
 import jax.numpy as jnp
@@ -23,20 +24,32 @@
     return first, second, third
 
 
-def side_columns(value):
-    lane = lax.broadcasted_iota(jnp.int32, value.shape, 1)
-    first, second, third = (p.astype(jnp.float32) for p in pieces(value))
-    zero = jnp.zeros_like(value)
-    picked = jnp.where(lane == 0, first, jnp.where(lane == 1, second, jnp.where(lane == 2, third, zero)))
-    return picked.astype(jnp.bfloat16)
+def side_columns(row):
+    first, second, third = (p.astype(jnp.float32) for p in pieces(jnp.broadcast_to(row, (8, LANES))))
+    line = lax.broadcasted_iota(jnp.int32, (8, LANES), 0)
+    zero = jnp.zeros_like(first)
+    eight = jnp.where(line == 0, first, jnp.where(line == 1, second, jnp.where(line == 2, third, zero)))
+    rest = jnp.zeros((LANES - 8, LANES), jnp.float32)
+    return jnp.concatenate([eight, rest], axis=0).T.astype(jnp.bfloat16)
 
 
 def column(row):
     return jnp.broadcast_to(row, (LANES, LANES)).T
 
 
+def unrolled(start, stop, body, most=4):
+    width = math.gcd(stop - start, most)
+
+    def step(i, unused):
+        for u in range(width):
+            body(start + i * width + u)
+        return unused
+
+    lax.fori_loop(0, (stop - start) // width, step, 0)
+
+
 def kernel(
-    C, D, x_ref, c_ref, p_ref, out_ref, lp_ref,
+    C, D, x_hbm, c_hbm, p_hbm, out_ref, lp_ref, x_ref, c_ref, p_ref, in_sem,
     caug, e_ref, xw, score_a, score_b, m_ref, sn_ref, stats, own, send_a, recv_a, recv_b,
     stat_send, stat_recv, a_send, a_recv, b_send, b_recv, c_send, c_recv,
 ):
@@ -51,6 +64,12 @@
     def far(q):
         return lax.rem(mine_x + q, X) * 2 + core
 
+    p_copy = pltpu.make_async_copy(p_hbm, p_ref, in_sem.at[0])
+    c_copy_in = pltpu.make_async_copy(c_hbm, c_ref, in_sem.at[1])
+    x_copy = pltpu.make_async_copy(x_hbm, x_ref, in_sem.at[2])
+    for copy in (p_copy, c_copy_in, x_copy):
+        copy.start()
+
     barrier = pltpu.get_barrier_semaphore()
 
     def greet(q, unused):
@@ -64,16 +83,17 @@
     for q in range(1, X):
         pl.semaphore_signal(barrier, inc=1, device_id={"dp": far(q)}, device_id_type=MESH)
 
-    def widen(b, unused):
+    def widen(b):
         rows = pl.ds(pl.multiple_of(b * LANES, LANES), LANES)
         c = c_ref[rows, :].astype(jnp.float32)
-        norm = jnp.sum(c * c, axis=1, keepdims=True)
-        bias = column(p_ref[pl.ds(b, 1), :]) - norm * BETA
+        norm = jnp.sum((c * c).T, axis=0, keepdims=True)
         caug[rows, :LANES] = (c * (2.0 * BETA)).astype(jnp.bfloat16)
-        caug[rows, LANES:] = side_columns(bias)
-        return unused
-
-    lax.fori_loop(0, k // LANES, widen, 0)
+        caug[rows, LANES:] = side_columns(p_ref[pl.ds(b, 1), :] - norm * BETA)
+
+    p_copy.wait()
+    c_copy_in.wait()
+    unrolled(0, k // LANES, widen)
+    x_copy.wait()
 
     KB = min(512, k)
     steps = n // COLS
@@ -174,26 +194,30 @@
         lp_ref[rows, :] = lse - sn_ref[rows, :] * BETA
         m_ref[rows, :] = jnp.exp(m_ref[rows, :] - lse)
 
-        def scale(r, unused):
+        def scale(r):
             at = pl.ds(pl.multiple_of(r * LANES, LANES), LANES)
             w = column(m_ref[pl.ds(r, 1), :])
             xw[at, :LANES] = (x_ref[at, :].astype(jnp.float32) * w).astype(jnp.bfloat16)
-            xw[at, LANES:] = side_columns(w)
-            return unused
-
-        lax.fori_loop(g * GR, (g + 1) * GR, scale, 0)
-
-    def partial(chunk, ref, i):
-        rows = pl.ds(pl.multiple_of(chunk * CHUNK, CHUNK), CHUNK)
-        s = jnp.dot(e_ref[rows, :], xw[...], preferred_element_type=jnp.float32)
-        ref[i, :CHUNK, :] = s[:, :LANES]
-        masses = jnp.zeros((8, LANES), jnp.float32)
+            xw[at, LANES:] = side_columns(m_ref[pl.ds(r, 1), :])
+
+        unrolled(g * GR, (g + 1) * GR, scale)
+
+    def partial(i):
+        theirs, mine = (
+            e_ref[pl.ds(pl.multiple_of((half * H + i) * CHUNK, CHUNK), CHUNK), :] for half in (1 - core, core)
+        )
+        both = jnp.dot(
+            jnp.concatenate([theirs, mine], axis=0), xw[...], preferred_element_type=jnp.float32
+        )
         line = lax.broadcasted_iota(jnp.int32, (8, LANES), 0)
-        for b in range(CHUNK // LANES):
-            t = s[b * LANES:(b + 1) * LANES, LANES:].T
-            row = jnp.sum(t[0:8, :], axis=0, keepdims=True)
-            masses = jnp.where(line == b, jnp.broadcast_to(row, (8, LANES)), masses)
-        ref[i, CHUNK:, :] = masses
+        for ref, s in ((send_a, both[:CHUNK]), (own, both[CHUNK:])):
+            ref[i, :CHUNK, :] = s[:, :LANES]
+            masses = jnp.zeros((8, LANES), jnp.float32)
+            for b in range(CHUNK // LANES):
+                t = s[b * LANES:(b + 1) * LANES, LANES:].T
+                row = jnp.sum(t[0:8, :], axis=0, keepdims=True)
+                masses = jnp.where(line == b, jnp.broadcast_to(row, (8, LANES)), masses)
+            ref[i, CHUNK:, :] = masses
 
     def a_copy(i):
         return pltpu.make_async_remote_copy(
@@ -222,9 +246,8 @@
             b_copy(q, i).start()
 
     def produce(i, unused):
-        partial((1 - core) * H + i, send_a, i)
+        partial(i)
         a_copy(i).start()
-        partial(core * H + i, own, i)
         chip_sum(i)
         return unused
 
@@ -275,9 +298,13 @@
                 jax.ShapeDtypeStruct((2 * H,) + chunk, f32),
                 jax.ShapeDtypeStruct((R, LANES), f32),
             ),
-            in_specs=[vmem] * 3,
+            in_specs=[pl.BlockSpec(memory_space=pltpu.HBM)] * 3,
             out_specs=(vmem, vmem),
             scratch_shapes=[
+                pltpu.VMEM((n, LANES), bf16),
+                pltpu.VMEM((k, LANES), bf16),
+                pltpu.VMEM((k // LANES, LANES), f32),
+                dma((3,)),
                 pltpu.VMEM((k, 2 * LANES), bf16),
                 pltpu.VMEM((k, n), bf16),
                 pltpu.VMEM((n, 2 * LANES), bf16),

time: 48.2 us -> 46.6 us (0.967)
  Pallas kernels: 42.1 us -> 40.5 us
    pallas_call x1, Pallas kernels: 42.1 us -> 40.5 us  [shards(): pl.pallas_call(functools.partial(kernel, C, D), out_shape=(jax.ShapeDtype...]
where the time goes in v2:
time: 46.6 us; the launch traced here: 46.3 us
  Pallas kernels  40.5 us (87%)
  local copies, waits for them, and re-layouts  5.2 us (11%)
  between operations  0.65 us (1%)
    pallas_call x1, Pallas kernels, shards(): pl.pallas_call(functools.partial(kernel, C, D), out_shape=(jax.ShapeDtype...  40.5 us
    unnamed x7, local copies, waits for them, and re-layouts  3.56 us
    slice x1, local copies, waits for them, and re-layouts, shards(): new_centres = out[:, :CHUNK, :].reshape(k, LANES)  1.04 us

profile of v2, /device:TPU:0, one launch (start us, length us, event | category | flops | bytes accessed | tf_op | source)
XLA Modules:
  0.0 46.3 jit_solution(3377070159626627429)
XLA Ops:
  0.6 0.0 copy-start
  0.6 1.2 %copy-done = bf16[4096,128]{1,0:T(8,128)(2,1)S(1)} copy-done((bf16[4096,128]{1,0:T(8,128)(2,1)S(1)}, bf16[4096,128]{1,0:T(8,128)(2,1)}, u32[]{:S(2)}) %copy-start) | copy-done | bytes 1048600
  1.9 0.0 copy-start.1
  1.9 1.0 %copy-done.1 = bf16[2048,128]{1,0:T(8,128)(2,1)S(1)} copy-done((bf16[2048,128]{1,0:T(8,128)(2,1)S(1)}, bf16[2048,128]{1,0:T(8,128)(2,1)}, u32[]{:S(2)}) %copy-start.1) | copy-done | bytes 524312
  2.9 0.0 copy-start.2
  2.9 0.7 %copy-done.2 = f32[2048]{0:T(1024)S(1)} copy-done((f32[2048]{0:T(1024)S(1)}, f32[2048]{0:T(1024)}, u32[]{:S(2)}) %copy-start.2) | copy-done | bytes 8216
  3.6 40.5 %shard_map.58 = (f32[8,264,128]{2,1,0:T(8,128)S(1)}, f32[32,128]{1,0:T(8,128)S(1)}) custom-call(bf16[4096,128]{1,0:T(8,128)(2,1)S(1)} %copy-done, bf16[2048,128]{1,0:T(8,128)(2,1)S(1)} %copy-done.1, f32[16,128]{1,0:T(8,128)S(1)} %bitcast.5), custom_call_target="tpu_custom_call" | custom-call | flops 8589934592 | bytes 2097152 | tf_op jit(solution)/shard_map/pallas_call | solution.py:295
  44.1 0.6 %slice.7 = f32[8,2,128]{2,1,0:T(2,128)} slice(f32[8,264,128]{2,1,0:T(8,128)S(1)} %get-tuple-element.5), slice={[0:8], [256:258], [0:128]} | slice | bytes 16384 | tf_op jit(solution)/shard_map/slice | solution.py:333
  44.7 1.0 %slice.6 = f32[8,256,128]{2,1,0:T(8,128)} slice(f32[8,264,128]{2,1,0:T(8,128)S(1)} %get-tuple-element.5), slice={[0:8], [0:256], [0:128]} | slice | bytes 2097152 | tf_op jit(solution)/shard_map/slice | solution.py:332
  45.7 0.6 %copy.7 = f32[4096]{0:T(1024)} copy(f32[4096]{0:T(1024)S(1)} %bitcast.4) | data formatting | bytes 32768
Async XLA Ops:
  0.6 1.2 %copy-start = (bf16[4096,128]{1,0:T(8,128)(2,1)S(1)}, bf16[4096,128]{1,0:T(8,128)(2,1)}, u32[]{:S(2)}) copy-start(bf16[4096,128]{1,0:T(8,128)(2,1)} %x_hbm.1) | copy-start | bytes 3145732
  1.9 1.0 %copy-start.1 = (bf16[2048,128]{1,0:T(8,128)(2,1)S(1)}, bf16[2048,128]{1,0:T(8,128)(2,1)}, u32[]{:S(2)}) copy-start(bf16[2048,128]{1,0:T(8,128)(2,1)} %c_hbm.1) | copy-start | bytes 1572868
  2.9 0.7 %copy-start.2 = (f32[2048]{0:T(1024)S(1)}, f32[2048]{0:T(1024)}, u32[]{:S(2)}) copy-start(f32[2048]{0:T(1024)} %param.5) | copy-start | bytes 24580

commit v3 on v2

--- a/solution.py
+++ b/solution.py
@@ -13,7 +13,7 @@
 LANES = 128
 COLS = 256
 MOST = 256
-GROUPS = 2
+GROUPS = 4
 
 
 def pieces(value):

time: 46.6 us -> 46.6 us (level)
  no operation moved by 1% of the time
where the time goes in v3:
time: 46.6 us; the launch traced here: 46.3 us
  Pallas kernels  40.5 us (87%)
  local copies, waits for them, and re-layouts  5.2 us (11%)
  between operations  0.65 us (1%)
    pallas_call x1, Pallas kernels, shards(): pl.pallas_call(functools.partial(kernel, C, D), out_shape=(jax.ShapeDtype...  40.5 us
    unnamed x7, local copies, waits for them, and re-layouts  3.56 us
    slice x1, local copies, waits for them, and re-layouts, shards(): new_centres = out[:, :CHUNK, :].reshape(k, LANES)  1.04 us

profile of v3, /device:TPU:0, one launch (start us, length us, event | category | flops | bytes accessed | tf_op | source)
XLA Modules:
  0.0 46.3 jit_solution(4310029523070181812)
XLA Ops:
  0.6 0.0 copy-start
  0.6 1.2 %copy-done = bf16[4096,128]{1,0:T(8,128)(2,1)S(1)} copy-done((bf16[4096,128]{1,0:T(8,128)(2,1)S(1)}, bf16[4096,128]{1,0:T(8,128)(2,1)}, u32[]{:S(2)}) %copy-start) | copy-done | bytes 1048600
  1.9 0.0 copy-start.1
  1.9 1.0 %copy-done.1 = bf16[2048,128]{1,0:T(8,128)(2,1)S(1)} copy-done((bf16[2048,128]{1,0:T(8,128)(2,1)S(1)}, bf16[2048,128]{1,0:T(8,128)(2,1)}, u32[]{:S(2)}) %copy-start.1) | copy-done | bytes 524312
  2.9 0.0 copy-start.2
  2.9 0.7 %copy-done.2 = f32[2048]{0:T(1024)S(1)} copy-done((f32[2048]{0:T(1024)S(1)}, f32[2048]{0:T(1024)}, u32[]{:S(2)}) %copy-start.2) | copy-done | bytes 8216
  3.6 40.5 %shard_map.58 = (f32[8,264,128]{2,1,0:T(8,128)S(1)}, f32[32,128]{1,0:T(8,128)S(1)}) custom-call(bf16[4096,128]{1,0:T(8,128)(2,1)S(1)} %copy-done, bf16[2048,128]{1,0:T(8,128)(2,1)S(1)} %copy-done.1, f32[16,128]{1,0:T(8,128)S(1)} %bitcast.5), custom_call_target="tpu_custom_call" | custom-call | flops 8589934592 | bytes 2097152 | tf_op jit(solution)/shard_map/pallas_call | solution.py:295
  44.1 0.6 %slice.7 = f32[8,2,128]{2,1,0:T(2,128)} slice(f32[8,264,128]{2,1,0:T(8,128)S(1)} %get-tuple-element.5), slice={[0:8], [256:258], [0:128]} | slice | bytes 16384 | tf_op jit(solution)/shard_map/slice | solution.py:333
  44.7 1.0 %slice.6 = f32[8,256,128]{2,1,0:T(8,128)} slice(f32[8,264,128]{2,1,0:T(8,128)S(1)} %get-tuple-element.5), slice={[0:8], [0:256], [0:128]} | slice | bytes 2097152 | tf_op jit(solution)/shard_map/slice | solution.py:332
  45.7 0.6 %copy.7 = f32[4096]{0:T(1024)} copy(f32[4096]{0:T(1024)S(1)} %bitcast.4) | data formatting | bytes 32768
Async XLA Ops:
  0.6 1.2 %copy-start = (bf16[4096,128]{1,0:T(8,128)(2,1)S(1)}, bf16[4096,128]{1,0:T(8,128)(2,1)}, u32[]{:S(2)}) copy-start(bf16[4096,128]{1,0:T(8,128)(2,1)} %x_hbm.1) | copy-start | bytes 3145732
  1.9 1.0 %copy-start.1 = (bf16[2048,128]{1,0:T(8,128)(2,1)S(1)}, bf16[2048,128]{1,0:T(8,128)(2,1)}, u32[]{:S(2)}) copy-start(bf16[2048,128]{1,0:T(8,128)(2,1)} %c_hbm.1) | copy-start | bytes 1572868
  2.9 0.7 %copy-start.2 = (f32[2048]{0:T(1024)S(1)}, f32[2048]{0:T(1024)}, u32[]{:S(2)}) copy-start(f32[2048]{0:T(1024)} %param.5) | copy-start | bytes 24580

commit v4 on v2

--- a/solution.py
+++ b/solution.py
@@ -248,10 +248,15 @@
     def produce(i, unused):
         partial(i)
         a_copy(i).start()
-        chip_sum(i)
+
+        @pl.when(i > 0)
+        def behind():
+            chip_sum(i - 1)
+
         return unused
 
     lax.fori_loop(0, H, produce, 0)
+    chip_sum(H - 1)
 
     denominator = float(n * D + k * C)
 

time: 46.6 us -> 46.6 us (level)
  no operation moved by 1% of the time
where the time goes in v4:
time: 46.6 us; the launch traced here: 46.3 us
  Pallas kernels  40.5 us (87%)
  local copies, waits for them, and re-layouts  5.2 us (11%)
  between operations  0.65 us (1%)
    pallas_call x1, Pallas kernels, shards(): pl.pallas_call(functools.partial(kernel, C, D), out_shape=(jax.ShapeDtype...  40.5 us
    unnamed x7, local copies, waits for them, and re-layouts  3.56 us
    slice x1, local copies, waits for them, and re-layouts, shards(): new_centres = out[:, :CHUNK, :].reshape(k, LANES)  1.04 us

profile of v4, /device:TPU:0, one launch (start us, length us, event | category | flops | bytes accessed | tf_op | source)
XLA Modules:
  0.0 46.3 jit_solution(16906191508305187151)
XLA Ops:
  0.6 0.0 copy-start
  0.6 1.2 %copy-done = bf16[4096,128]{1,0:T(8,128)(2,1)S(1)} copy-done((bf16[4096,128]{1,0:T(8,128)(2,1)S(1)}, bf16[4096,128]{1,0:T(8,128)(2,1)}, u32[]{:S(2)}) %copy-start) | copy-done | bytes 1048600
  1.9 0.0 copy-start.1
  1.9 1.0 %copy-done.1 = bf16[2048,128]{1,0:T(8,128)(2,1)S(1)} copy-done((bf16[2048,128]{1,0:T(8,128)(2,1)S(1)}, bf16[2048,128]{1,0:T(8,128)(2,1)}, u32[]{:S(2)}) %copy-start.1) | copy-done | bytes 524312
  2.9 0.0 copy-start.2
  2.9 0.7 %copy-done.2 = f32[2048]{0:T(1024)S(1)} copy-done((f32[2048]{0:T(1024)S(1)}, f32[2048]{0:T(1024)}, u32[]{:S(2)}) %copy-start.2) | copy-done | bytes 8216
  3.6 40.5 %shard_map.58 = (f32[8,264,128]{2,1,0:T(8,128)S(1)}, f32[32,128]{1,0:T(8,128)S(1)}) custom-call(bf16[4096,128]{1,0:T(8,128)(2,1)S(1)} %copy-done, bf16[2048,128]{1,0:T(8,128)(2,1)S(1)} %copy-done.1, f32[16,128]{1,0:T(8,128)S(1)} %bitcast.5), custom_call_target="tpu_custom_call" | custom-call | flops 8589934592 | bytes 2097152 | tf_op jit(solution)/shard_map/pallas_call | solution.py:300
  44.1 0.6 %slice.7 = f32[8,2,128]{2,1,0:T(2,128)} slice(f32[8,264,128]{2,1,0:T(8,128)S(1)} %get-tuple-element.5), slice={[0:8], [256:258], [0:128]} | slice | bytes 16384 | tf_op jit(solution)/shard_map/slice | solution.py:338
  44.7 1.0 %slice.6 = f32[8,256,128]{2,1,0:T(8,128)} slice(f32[8,264,128]{2,1,0:T(8,128)S(1)} %get-tuple-element.5), slice={[0:8], [0:256], [0:128]} | slice | bytes 2097152 | tf_op jit(solution)/shard_map/slice | solution.py:337
  45.7 0.6 %copy.7 = f32[4096]{0:T(1024)} copy(f32[4096]{0:T(1024)S(1)} %bitcast.4) | data formatting | bytes 32768
Async XLA Ops:
  0.6 1.2 %copy-start = (bf16[4096,128]{1,0:T(8,128)(2,1)S(1)}, bf16[4096,128]{1,0:T(8,128)(2,1)}, u32[]{:S(2)}) copy-start(bf16[4096,128]{1,0:T(8,128)(2,1)} %x_hbm.1) | copy-start | bytes 3145732
  1.9 1.0 %copy-start.1 = (bf16[2048,128]{1,0:T(8,128)(2,1)S(1)}, bf16[2048,128]{1,0:T(8,128)(2,1)}, u32[]{:S(2)}) copy-start(bf16[2048,128]{1,0:T(8,128)(2,1)} %c_hbm.1) | copy-start | bytes 1572868
  2.9 0.7 %copy-start.2 = (f32[2048]{0:T(1024)S(1)}, f32[2048]{0:T(1024)}, u32[]{:S(2)}) copy-start(f32[2048]{0:T(1024)} %param.5) | copy-start | bytes 24580

commit v5 on v4

--- a/solution.py
+++ b/solution.py
@@ -60,6 +60,11 @@
     me_c, me_d = lax.axis_index("centre"), lax.axis_index("dp")
     core, mine_x = lax.rem(me_d, 2), lax.div(me_d, 2)
     sibling = mine_x * 2 + (1 - core)
+    Q = C // 2
+    half_c, par_c = lax.div(me_c, 2), lax.rem(me_c, 2)
+
+    def peer(q):
+        return jnp.where(q == 0, half_c * 2 + (1 - par_c), lax.rem(half_c + q, Q) * 2 + par_c)
 
     def far(q):
         return lax.rem(mine_x + q, X) * 2 + core
@@ -74,11 +79,11 @@
 
     def greet(q, unused):
         pl.semaphore_signal(
-            barrier, inc=1, device_id={"centre": lax.rem(me_c + q, C)}, device_id_type=MESH
-        )
-        return unused
-
-    lax.fori_loop(1, C, greet, 0)
+            barrier, inc=1, device_id={"centre": peer(q)}, device_id_type=MESH
+        )
+        return unused
+
+    lax.fori_loop(0, Q, greet, 0)
     pl.semaphore_signal(barrier, inc=1, device_id={"dp": sibling}, device_id_type=MESH)
     for q in range(1, X):
         pl.semaphore_signal(barrier, inc=1, device_id={"dp": far(q)}, device_id_type=MESH)
@@ -145,7 +150,7 @@
             part = slice(b * LANES, (b + 1) * LANES)
             m_ref[row, :] = m[:, part]
             sn_ref[row, :] = norm[:, part]
-            stats[0, row, :] = lse[:, part]
+            stats[Q, row, :] = lse[:, part]
         return jnp.max(top, axis=0, keepdims=True)
 
     def pair(i, m):
@@ -155,39 +160,58 @@
     R = n // LANES
     GR = R // GROUPS
 
+    def pair_copy(g):
+        rows = slice(g * GR, (g + 1) * GR)
+        return pltpu.make_async_remote_copy(
+            src_ref=stats.at[Q, rows], dst_ref=stats.at[Q + 1, rows],
+            send_sem=stat_send.at[g, 0], recv_sem=stat_recv.at[g, 0],
+            device_id={"centre": half_c * 2 + (1 - par_c)}, device_id_type=MESH,
+        )
+
     def stat_copy(g, q):
         rows = slice(g * GR, (g + 1) * GR)
         return pltpu.make_async_remote_copy(
             src_ref=stats.at[0, rows], dst_ref=stats.at[q, rows],
             send_sem=stat_send.at[g, q], recv_sem=stat_recv.at[g, q],
-            device_id={"centre": lax.rem(me_c + q, C)}, device_id_type=MESH,
-        )
+            device_id={"centre": lax.rem(half_c + q, Q) * 2 + par_c}, device_id_type=MESH,
+        )
+
+    def pass_on(g):
+        pair_copy(g).wait()
+        rows = slice(g * GR, (g + 1) * GR)
+        mine, theirs = stats[Q, rows, :], stats[Q + 1, rows, :]
+        top = jnp.maximum(mine, theirs)
+        stats[0, rows, :] = top + jnp.log(jnp.exp(mine - top) + jnp.exp(theirs - top))
+
+        def send(q, unused):
+            stat_copy(g, q).start()
+            return unused
+
+        lax.fori_loop(1, Q, send, 0)
 
     m = first_scores(score_a, 0)
     per_group = steps // 2 // GROUPS
     for g in range(GROUPS):
         m = lax.fori_loop(g * per_group, (g + 1) * per_group, pair, m)
         if g == 0:
-            pl.semaphore_wait(barrier, C - 1 + 1 + X - 1)
-
-        def send(q, unused, g=g):
-            stat_copy(g, q).start()
-            return unused
-
-        lax.fori_loop(1, C, send, 0)
+            pl.semaphore_wait(barrier, Q + X)
+        pair_copy(g).start()
+        if g > 0:
+            pass_on(g - 1)
+    pass_on(GROUPS - 1)
 
     for g in range(GROUPS):
         def arrive(q, unused, g=g):
             stat_copy(g, q).wait()
             return unused
 
-        lax.fori_loop(1, C, arrive, 0)
+        lax.fori_loop(1, Q, arrive, 0)
         rows = slice(g * GR, (g + 1) * GR)
         top = lax.fori_loop(
-            1, C, lambda q, t, rows=rows: jnp.maximum(t, stats[q, rows, :]), stats[0, rows, :]
+            1, Q, lambda q, t, rows=rows: jnp.maximum(t, stats[q, rows, :]), stats[0, rows, :]
         )
         total = lax.fori_loop(
-            0, C, lambda q, t, rows=rows, top=top: t + jnp.exp(stats[q, rows, :] - top),
+            0, Q, lambda q, t, rows=rows, top=top: t + jnp.exp(stats[q, rows, :] - top),
             jnp.zeros_like(top),
         )
         lse = top + jnp.log(total)
@@ -317,12 +341,12 @@
                 pltpu.VMEM((k, COLS), f32),
                 pltpu.VMEM((R, LANES), f32),
                 pltpu.VMEM((R, LANES), f32),
-                pltpu.VMEM((C, R, LANES), f32),
+                pltpu.VMEM((C // 2 + 2, R, LANES), f32),
                 pltpu.VMEM((H,) + chunk, f32),
                 pltpu.VMEM((H,) + chunk, f32),
                 pltpu.VMEM((H,) + chunk, f32),
                 pltpu.VMEM((max(X - 1, 1), H) + chunk, f32),
-                dma((GROUPS, C)), dma((GROUPS, C)),
+                dma((GROUPS, C // 2)), dma((GROUPS, C // 2)),
                 dma((H,)), dma((H,)),
                 dma((max(X - 1, 1), H)), dma((max(X - 1, 1), H)),
                 dma((H,)), dma((H,)),

time: 46.6 us -> 48.4 us (1.039)
  Pallas kernels: 40.5 us -> 42.3 us
    pallas_call x1, Pallas kernels: 40.5 us -> 42.3 us  [shards(): pl.pallas_call(functools.partial(kernel, C, D), out_shape=(jax.ShapeDtype...]
where the time goes in v5:
time: 48.4 us; the launch traced here: 48.2 us
  Pallas kernels  42.3 us (87%)
  local copies, waits for them, and re-layouts  5.2 us (11%)
  between operations  0.65 us (1%)
    pallas_call x1, Pallas kernels, shards(): pl.pallas_call(functools.partial(kernel, C, D), out_shape=(jax.ShapeDtype...  42.3 us
    unnamed x7, local copies, waits for them, and re-layouts  3.56 us
    slice x1, local copies, waits for them, and re-layouts, shards(): new_centres = out[:, :CHUNK, :].reshape(k, LANES)  1.04 us

profile of v5, /device:TPU:0, one launch (start us, length us, event | category | flops | bytes accessed | tf_op | source)
XLA Modules:
  0.0 48.2 jit_solution(7789543622528565438)
XLA Ops:
  0.6 0.0 copy-start
  0.6 1.2 %copy-done = bf16[4096,128]{1,0:T(8,128)(2,1)S(1)} copy-done((bf16[4096,128]{1,0:T(8,128)(2,1)S(1)}, bf16[4096,128]{1,0:T(8,128)(2,1)}, u32[]{:S(2)}) %copy-start) | copy-done | bytes 1048600
  1.9 0.0 copy-start.1
  1.9 1.0 %copy-done.1 = bf16[2048,128]{1,0:T(8,128)(2,1)S(1)} copy-done((bf16[2048,128]{1,0:T(8,128)(2,1)S(1)}, bf16[2048,128]{1,0:T(8,128)(2,1)}, u32[]{:S(2)}) %copy-start.1) | copy-done | bytes 524312
  2.9 0.0 copy-start.2
  2.9 0.7 %copy-done.2 = f32[2048]{0:T(1024)S(1)} copy-done((f32[2048]{0:T(1024)S(1)}, f32[2048]{0:T(1024)}, u32[]{:S(2)}) %copy-start.2) | copy-done | bytes 8216
  3.6 42.3 %shard_map.58 = (f32[8,264,128]{2,1,0:T(8,128)S(1)}, f32[32,128]{1,0:T(8,128)S(1)}) custom-call(bf16[4096,128]{1,0:T(8,128)(2,1)S(1)} %copy-done, bf16[2048,128]{1,0:T(8,128)(2,1)S(1)} %copy-done.1, f32[16,128]{1,0:T(8,128)S(1)} %bitcast.5), custom_call_target="tpu_custom_call" | custom-call | flops 8589934592 | bytes 2097152 | tf_op jit(solution)/shard_map/pallas_call | solution.py:324
  45.9 0.6 %slice.7 = f32[8,2,128]{2,1,0:T(2,128)} slice(f32[8,264,128]{2,1,0:T(8,128)S(1)} %get-tuple-element.5), slice={[0:8], [256:258], [0:128]} | slice | bytes 16384 | tf_op jit(solution)/shard_map/slice | solution.py:362
  46.5 1.0 %slice.6 = f32[8,256,128]{2,1,0:T(8,128)} slice(f32[8,264,128]{2,1,0:T(8,128)S(1)} %get-tuple-element.5), slice={[0:8], [0:256], [0:128]} | slice | bytes 2097152 | tf_op jit(solution)/shard_map/slice | solution.py:361
  47.5 0.6 %copy.7 = f32[4096]{0:T(1024)} copy(f32[4096]{0:T(1024)S(1)} %bitcast.4) | data formatting | bytes 32768
Async XLA Ops:
  0.6 1.2 %copy-start = (bf16[4096,128]{1,0:T(8,128)(2,1)S(1)}, bf16[4096,128]{1,0:T(8,128)(2,1)}, u32[]{:S(2)}) copy-start(bf16[4096,128]{1,0:T(8,128)(2,1)} %x_hbm.1) | copy-start | bytes 3145732
  1.9 1.0 %copy-start.1 = (bf16[2048,128]{1,0:T(8,128)(2,1)S(1)}, bf16[2048,128]{1,0:T(8,128)(2,1)}, u32[]{:S(2)}) copy-start(bf16[2048,128]{1,0:T(8,128)(2,1)} %c_hbm.1) | copy-start | bytes 1572868
  2.9 0.7 %copy-start.2 = (f32[2048]{0:T(1024)S(1)}, f32[2048]{0:T(1024)}, u32[]{:S(2)}) copy-start(f32[2048]{0:T(1024)} %param.5) | copy-start | bytes 24580

commit v6 on v4

--- a/solution.py
+++ b/solution.py
@@ -12,7 +12,7 @@
 BETA = 0.0625
 LANES = 128
 COLS = 256
-MOST = 256
+MOST = 128
 GROUPS = 2
 
 

time: 46.6 us -> 46.5 us (level)
  no operation moved by 1% of the time
where the time goes in v6:
time: 46.5 us; the launch traced here: 46.2 us
  Pallas kernels  40.3 us (87%)
  local copies, waits for them, and re-layouts  5.24 us (11%)
  between operations  0.65 us (1%)
    pallas_call x1, Pallas kernels, shards(): pl.pallas_call(functools.partial(kernel, C, D), out_shape=(jax.ShapeDtype...  40.3 us
    unnamed x7, local copies, waits for them, and re-layouts  3.56 us
    slice x1, local copies, waits for them, and re-layouts, shards(): new_centres = out[:, :CHUNK, :].reshape(k, LANES)  1.08 us

profile of v6, /device:TPU:0, one launch (start us, length us, event | category | flops | bytes accessed | tf_op | source)
XLA Modules:
  0.0 46.2 jit_solution(1008259980519573631)
XLA Ops:
  0.6 0.0 copy-start
  0.6 1.2 %copy-done = bf16[4096,128]{1,0:T(8,128)(2,1)S(1)} copy-done((bf16[4096,128]{1,0:T(8,128)(2,1)S(1)}, bf16[4096,128]{1,0:T(8,128)(2,1)}, u32[]{:S(2)}) %copy-start) | copy-done | bytes 1048600
  1.9 0.0 copy-start.1
  1.9 1.0 %copy-done.1 = bf16[2048,128]{1,0:T(8,128)(2,1)S(1)} copy-done((bf16[2048,128]{1,0:T(8,128)(2,1)S(1)}, bf16[2048,128]{1,0:T(8,128)(2,1)}, u32[]{:S(2)}) %copy-start.1) | copy-done | bytes 524312
  2.9 0.0 copy-start.2
  2.9 0.7 %copy-done.2 = f32[2048]{0:T(1024)S(1)} copy-done((f32[2048]{0:T(1024)S(1)}, f32[2048]{0:T(1024)}, u32[]{:S(2)}) %copy-start.2) | copy-done | bytes 8216
  3.6 40.3 %shard_map.58 = (f32[16,136,128]{2,1,0:T(8,128)S(1)}, f32[32,128]{1,0:T(8,128)S(1)}) custom-call(bf16[4096,128]{1,0:T(8,128)(2,1)S(1)} %copy-done, bf16[2048,128]{1,0:T(8,128)(2,1)S(1)} %copy-done.1, f32[16,128]{1,0:T(8,128)S(1)} %bitcast.5), custom_call_target="tpu_custom_call" | custom-call | flops 8589934592 | bytes 2097152 | tf_op jit(solution)/shard_map/pallas_call | solution.py:300
  43.9 0.6 %slice.7 = f32[16,1,128]{2,1,0:T(1,128)} slice(f32[16,136,128]{2,1,0:T(8,128)S(1)} %get-tuple-element.5), slice={[0:16], [128:129], [0:128]} | slice | bytes 16384 | tf_op jit(solution)/shard_map/slice | solution.py:338
  44.5 1.1 %slice.6 = f32[16,128,128]{2,1,0:T(8,128)} slice(f32[16,136,128]{2,1,0:T(8,128)S(1)} %get-tuple-element.5), slice={[0:16], [0:128], [0:128]} | slice | bytes 2097152 | tf_op jit(solution)/shard_map/slice | solution.py:337
  45.6 0.6 %copy.7 = f32[4096]{0:T(1024)} copy(f32[4096]{0:T(1024)S(1)} %bitcast.4) | data formatting | bytes 32768
Async XLA Ops:
  0.6 1.2 %copy-start = (bf16[4096,128]{1,0:T(8,128)(2,1)S(1)}, bf16[4096,128]{1,0:T(8,128)(2,1)}, u32[]{:S(2)}) copy-start(bf16[4096,128]{1,0:T(8,128)(2,1)} %x_hbm.1) | copy-start | bytes 3145732
  1.9 1.0 %copy-start.1 = (bf16[2048,128]{1,0:T(8,128)(2,1)S(1)}, bf16[2048,128]{1,0:T(8,128)(2,1)}, u32[]{:S(2)}) copy-start(bf16[2048,128]{1,0:T(8,128)(2,1)} %c_hbm.1) | copy-start | bytes 1572868
  2.9 0.7 %copy-start.2 = (f32[2048]{0:T(1024)S(1)}, f32[2048]{0:T(1024)}, u32[]{:S(2)}) copy-start(f32[2048]{0:T(1024)} %param.5) | copy-start | bytes 24580
